TPU v7x, 32 devices: a whole 2x2x4 slice. The times are simulated.
32 devices in a mesh: samples: 8 (over z, y), vblocks: 4 (over x, core).
Axes of the slice: x: 2, y: 2, z: 4, core: 2. Of those that a mesh axis runs over, the one named last changes fastest.
Arguments:
- genotypes: int32 [8192, 4096], P('samples', 'vblocks'), may hold values from 0 to 2
- typed_mask: int32 [4096], P('vblocks'), may hold values 0 or 1
- z_scores: float32 [128, 4096], P('samples', 'vblocks'), may hold values from -60 to 60
Outputs:
- solution: float32 [128, 4096], P('samples', 'vblocks')
- imputed: float32 [128, 4096], P('samples', 'vblocks')
All inputs are finite; a program needn't handle non-finite values. No bound on the sum of `typed_mask` on one device may be relied on, other than what follows from the above.
Results may differ from a plain program's by a relative error of at most 0.0068.
Values may be sent and summed in bfloat16 or wider, within the bound.
A program may use at most 64 MiB of HBM per device.

v0:
```python
import jax
import jax.numpy as jnp
from jax import lax
from jax.sharding import PartitionSpec as P

ITERS = 3


RIDGE = 0.1
EPSILON = 1e-05
HIGHEST = lax.Precision.HIGHEST


def passed_along(block, axis, distance):
    devices = range(lax.axis_size(axis))
    route = [(i - distance, i) for i in devices if i - distance in devices]
    return lax.ppermute(block, axis, route)


def contract_rows(first_mat, second_mat):
    return lax.dot_general(
        first_mat, second_mat, (((0,), (0,)), ((), ())), preferred_element_type=jnp.float32
    )


def times_transpose(vector, matrix):
    return lax.dot_general(
        vector,
        matrix,
        (((1,), (1,)), ((), ())),
        precision=HIGHEST,
        preferred_element_type=jnp.float32,
    )


def local_sums(first_vec, second_vec):
    return jnp.sum(first_vec * second_vec, axis=1)


def on_device(genotypes, typed_mask, z_scores):
    samples_dev, block_width = genotypes.shape
    total_samples = samples_dev * lax.axis_size("samples")
    dosage = genotypes.astype(jnp.float32)
    totals, squares = lax.psum(
        (jnp.sum(dosage, axis=0), jnp.sum(dosage * dosage, axis=0)), "samples"
    )
    mean_dosage = totals / total_samples
    variance = squares / total_samples - mean_dosage * mean_dosage
    standard = ((dosage - mean_dosage) * lax.rsqrt(variance + EPSILON)).astype(jnp.bfloat16)
    following = passed_along(standard, "vblocks", -1)
    joined = jnp.concatenate([standard, following], axis=1)
    summed = lax.psum_scatter(
        contract_rows(standard, joined), "samples", scatter_dimension=0, tiled=True
    )
    link_rows = (summed / total_samples).astype(jnp.bfloat16)
    gathered = lax.all_gather(link_rows, "samples", axis=0, tiled=True)
    own_block = gathered[:, :block_width].astype(jnp.float32)
    edge_half = gathered[:, block_width:]
    edge_block = edge_half.astype(jnp.float32)

    def apply_link(vector):
        ahead_part = passed_along(vector, "vblocks", -1)
        outgoing = jnp.dot(
            vector, edge_block, precision=HIGHEST, preferred_element_type=jnp.float32
        )
        lower_part = passed_along(outgoing, "vblocks", 1)
        result = times_transpose(vector, own_block)
        result = result + 0.5 * times_transpose(ahead_part, edge_block)
        return result + 0.5 * lower_part

    mask_row = typed_mask.astype(jnp.float32)[None, :]

    def operator(vector):
        return mask_row * apply_link(mask_row * vector) + RIDGE * vector

    right_side = mask_row * z_scores
    solution = jnp.zeros_like(right_side)
    residual = right_side

    def pair_sums(vector, image):
        return lax.psum((local_sums(vector, vector), local_sums(vector, image)), "vblocks")

    image = operator(residual)
    norm_now, product = pair_sums(residual, image)
    step_size = norm_now / product
    direction = residual
    along_dir = image
    for iteration in range(ITERS):
        solution = solution + step_size[:, None] * direction
        if iteration + 1 < ITERS:
            residual = residual - step_size[:, None] * along_dir
            image = operator(residual)
            norm_next, product = pair_sums(residual, image)
            beta_ratio = norm_next / norm_now
            step_size = norm_next / (product - beta_ratio * norm_next / step_size)
            direction = residual + beta_ratio[:, None] * direction
            along_dir = image + beta_ratio[:, None] * along_dir
            norm_now = norm_next
    projected = apply_link(mask_row * solution)
    imputed = jnp.where(typed_mask[None, :] == 1, z_scores, projected)
    return (solution, imputed)


def solution(mesh):
    placed = (P("samples", "vblocks"), P("vblocks"), P("samples", "vblocks"))
    return jax.shard_map(
        on_device,
        mesh=mesh,
        in_specs=placed,
        out_specs=(P("samples", "vblocks"), P("samples", "vblocks")),
        check_vma=False,
    )
```

profile of v0, /device:TPU:1, one launch (start us, length us, event | category | flops | bytes accessed | tf_op | source)
XLA Modules:
  0.0 367.3 jit_solution(12023599788768251750)
XLA Ops:
  7.2 0.0 reduce-scatter.2.cloned.1.call-start
  7.2 2.8 convert_reduce_fusion
  10.0 19.0 %all-reduce = (f32[1024]{0:T(1024)S(1)}, f32[1024]{0:T(1024)S(1)}) all-reduce(f32[1024]{0:T(1024)S(1)} %get-tuple-element.3, f32[1024]{0:T(1024)S(1)} %get-tuple-element.2), channel_id=1, replica_groups=mesh['samples'=8,'vblocks'=4] {'samples'}, use_global_device_ids=true, to_apply=%region_5.0 | all-reduce | flops 2048 | bytes 16384 | tf_op jit(solution)/shard_map/psum | solution.py:44
  29.0 2.8 multiply_convert_fusion
  31.8 6.3 %collective-permute-start = (bf16[1024,1024]{1,0:T(8,128)(2,1)S(1)}, bf16[1024,1024]{1,0:T(8,128)(2,1)S(1)}, u32[]{:S(2)}, u32[]{:S(2)}) collective-permute-start(bf16[1024,1024]{1,0:T(8,128)(2,1)S(1)} %multiply_convert_fusion), channel_id=1, source_target_pairs={{1,0},{2,1},{3,2},{5,4},{6,5},{7,6},{9,8},{10,9},{11,10},{13,12},{... | collective-permute-start | bytes 6291464 | tf_op jit(solution)/shard_map/ppermute | solution.py:17
  38.2 24.8 %collective-permute-done = bf16[1024,1024]{1,0:T(8,128)(2,1)S(1)} collective-permute-done((bf16[1024,1024]{1,0:T(8,128)(2,1)S(1)}, bf16[1024,1024]{1,0:T(8,128)(2,1)S(1)}, u32[]{:S(2)}, u32[]{:S(2)}) %collective-permute-start) | collective-permute-done | bytes 2097184 | tf_op jit(solution)/shard_map/ppermute | solution.py:17
  63.0 7.0 %fusion = f32[1024,2048]{1,0:T(8,128)} fusion(bf16[1024,1024]{1,0:T(8,128)(2,1)S(1)} %multiply_convert_fusion, bf16[1024,1024]{1,0:T(8,128)(2,1)S(1)} %collective-permute-done), kind=kOutput, calls=%fused_computation | convolution fusion | flops 4303355904 | bytes 12582912 | tf_op jit(solution)/shard_map/dot_general | solution.py:21
  70.0 0.0 copy-start.5
  70.0 0.0 copy-start.4
  70.0 0.0 reduce-scatter.2.cloned.1.call-update
  70.0 0.0 all-gather.2.cloned.1.call-start
  70.1 144.8 %reduce-scatter.2.cloned.1.call-done = f32[128,2048]{1,0:T(8,128)} async-done(((f32[1024,2048]{1,0:T(8,128)}), f32[128,2048]{1,0:T(8,128)}) %reduce-scatter.2.cloned.1.call-update) | async-done | bytes 1048592 | tf_op jit(solution)/shard_map/reduce_scatter | solution.py:52
  214.9 2.1 multiply_convert_fusion.1
  216.9 0.0 all-gather.2.cloned.1.call-update
  217.0 0.0 copy-done.5
  217.0 0.0 copy-done.4
  217.0 2.5 collective-permute-start.1
  219.6 68.8 %all-gather.2.cloned.1.call-done = bf16[1024,2048]{1,0:T(8,128)(2,1)} async-done(((bf16[128,2048]{1,0:T(8,128)(2,1)}), bf16[1024,2048]{1,0:T(8,128)(2,1)}) %all-gather.2.cloned.1.call-update) | async-done | bytes 4194320 | tf_op jit(solution)/shard_map/all_gather | solution.py:56
  288.4 0.0 copy-start
  288.4 2.7 fusion.38
  291.1 4.8 %collective-permute-start.2 = (f32[16,1024]{1,0:T(8,128)S(1)}, f32[16,1024]{1,0:T(8,128)S(1)}, u32[]{:S(2)}, u32[]{:S(2)}) collective-permute-start(f32[16,1024]{1,0:T(8,128)S(1)} %fusion.38), channel_id=1, source_target_pairs={{0,1},{1,2},{2,3},{4,5},{5,6},{6,7},{8,9},{9,10},{10,11},{12,13},{... | collective-permute-start | bytes 196616 | tf_op jit(solution)/shard_map/ppermute | solution.py:17
  295.9 3.3 fusion.10
  299.2 0.0 collective-permute-done.1
  299.2 0.0 collective-permute-done.2
  299.2 0.0 copy-done
  299.3 1.9 multiply_reduce_fusion.4
  301.1 5.1 %all-reduce.3 = (f32[16]{0:T(128)S(1)}, f32[16]{0:T(128)S(1)}) all-reduce(f32[16]{0:T(128)S(1)} %get-tuple-element.5, f32[16]{0:T(128)S(1)} %get-tuple-element.4), channel_id=1, replica_groups=mesh['samples'=8,'vblocks'=4] {'vblocks'}, use_global_device_ids=true, to_apply=%region_1.0 | all-reduce | flops 32 | bytes 256 | tf_op jit(solution)/shard_map/psum | solution.py:81
  306.2 0.0 copy-start.1
  306.2 0.1 broadcast_multiply_fusion.2
  306.3 3.2 collective-permute-start.3
  309.6 2.5 fusion.35
  312.1 3.1 collective-permute-start.4
  315.2 3.3 fusion.8
  318.6 0.0 collective-permute-done.4
  318.6 0.0 collective-permute-done.3
  318.6 0.0 copy-done.1
  318.6 1.9 multiply_reduce_fusion.2
  320.4 5.1 %all-reduce.2 = (f32[16]{0:T(128)S(1)}, f32[16]{0:T(128)S(1)}) all-reduce(f32[16]{0:T(128)S(1)} %get-tuple-element.7, f32[16]{0:T(128)S(1)} %get-tuple-element.6), channel_id=1, replica_groups=mesh['samples'=8,'vblocks'=4] {'vblocks'}, use_global_device_ids=true, to_apply=%region_10.0 | all-reduce | flops 32 | bytes 256 | tf_op jit(solution)/shard_map/psum | solution.py:81
  325.6 0.0 copy-start.2
  325.6 0.1 broadcast_multiply_fusion.1
  325.7 3.5 collective-permute-start.5
  329.2 2.5 fusion.32
  331.7 3.0 collective-permute-start.6
  334.8 3.3 fusion.6
  338.1 0.1 multiply_reduce_fusion.1
  338.2 0.0 collective-permute-done.6
  338.2 0.0 collective-permute-done.5
  338.2 0.0 copy-done.2
  338.2 1.9 fusion.28
  340.1 5.1 %all-reduce.1 = (f32[16]{0:T(128)S(1)}, f32[16]{0:T(128)S(1)}) all-reduce(f32[16]{0:T(128)S(1)} %multiply_reduce_fusion.1, f32[16]{0:T(128)S(1)} %fusion.28), channel_id=1, replica_groups=mesh['samples'=8,'vblocks'=4] {'vblocks'}, use_global_device_ids=true, to_apply=%region_14.0 | all-reduce | flops 32 | bytes 256 | tf_op jit(solution)/shard_map/psum | solution.py:81
  345.2 0.0 copy-start.3
  345.2 0.7 broadcast_multiply_fusion
  346.0 3.2 collective-permute-start.7
  349.1 2.5 fusion.29
  351.7 3.0 collective-permute-start.8
  354.7 3.3 fusion.4
  358.0 0.0 collective-permute-done.8
  358.0 0.0 collective-permute-done.7
  358.1 0.0 copy-done.3
  358.1 2.4 fusion.14
  (7 shorter events, 0.1 us)
Async XLA Ops:
  7.2 207.7 %reduce-scatter.2.cloned.1.call-start = ((), (), s32[]{:S(2)}) async-start(), calls=%async_computation.1 | async-start | bytes 9437184 | tf_op jit(solution)/shard_map/reduce_scatter | solution.py:52
  31.8 31.1 %collective-permute-start = (bf16[1024,1024]{1,0:T(8,128)(2,1)S(1)}, bf16[1024,1024]{1,0:T(8,128)(2,1)S(1)}, u32[]{:S(2)}, u32[]{:S(2)}) collective-permute-start(bf16[1024,1024]{1,0:T(8,128)(2,1)S(1)} %multiply_convert_fusion), channel_id=1, source_target_pairs={{1,0},{2,1},{3,2},{5,4},{6,5},{7,6},{9,8},{10,9},{11,10},{13,12},{... | collective-permute-start | bytes 6291464 | tf_op jit(solution)/shard_map/ppermute | solution.py:17
  70.0 147.0 %copy-start.5 = (s32[1024]{0:T(1024)S(1)}, s32[1024]{0:T(1024)}, u32[]{:S(2)}) copy-start(s32[1024]{0:T(1024)} %param.4) | copy-start | bytes 12292
  70.0 147.0 %copy-start.4 = (f32[16,1024]{1,0:T(8,128)S(1)}, f32[16,1024]{1,0:T(8,128)}, u32[]{:S(2)}) copy-start(f32[16,1024]{1,0:T(8,128)} %param.5) | copy-start | bytes 196612
  70.0 218.4 %all-gather.2.cloned.1.call-start = ((), (), s32[]{:S(2)}) async-start(), calls=%async_computation.2 | async-start | bytes 4718592 | tf_op jit(solution)/shard_map/all_gather | solution.py:56
  217.0 82.2 %collective-permute-start.1 = (f32[16,1024]{1,0:T(8,128)S(1)}, f32[16,1024]{1,0:T(8,128)S(1)}, u32[]{:S(2)}, u32[]{:S(2)}) collective-permute-start(f32[16,1024]{1,0:T(8,128)S(1)} %multiply_multiply_fusion), channel_id=1, source_target_pairs={{1,0},{2,1},{3,2},{5,4},{6,5},{7,6},{9,8},{10,9},{11,10},{13,12},{... | collective-permute-start | bytes 196616 | tf_op jit(solution)/shard_map/ppermute | solution.py:17
  288.4 10.9 %copy-start = (bf16[1024,2048]{1,0:T(8,128)(2,1)S(1)}, bf16[1024,2048]{1,0:T(8,128)(2,1)}, u32[]{:S(2)}) copy-start(bf16[1024,2048]{1,0:T(8,128)(2,1)} %all-gather.2.cloned.1.call-done) | copy-start | bytes 12582916
  291.1 8.2 %collective-permute-start.2 = (f32[16,1024]{1,0:T(8,128)S(1)}, f32[16,1024]{1,0:T(8,128)S(1)}, u32[]{:S(2)}, u32[]{:S(2)}) collective-permute-start(f32[16,1024]{1,0:T(8,128)S(1)} %fusion.38), channel_id=1, source_target_pairs={{0,1},{1,2},{2,3},{4,5},{5,6},{6,7},{8,9},{9,10},{10,11},{12,13},{... | collective-permute-start | bytes 196616 | tf_op jit(solution)/shard_map/ppermute | solution.py:17
  306.2 12.3 %copy-start.1 = (bf16[1024,2048]{1,0:T(8,128)(2,1)S(1)}, bf16[1024,2048]{1,0:T(8,128)(2,1)}, u32[]{:S(2)}) copy-start(bf16[1024,2048]{1,0:T(8,128)(2,1)} %all-gather.2.cloned.1.call-done) | copy-start | bytes 12582916
  306.3 12.2 %collective-permute-start.3 = (f32[16,1024]{1,0:T(8,128)S(1)}, f32[16,1024]{1,0:T(8,128)S(1)}, u32[]{:S(2)}, u32[]{:S(2)}) collective-permute-start(f32[16,1024]{1,0:T(8,128)S(1)} %get-tuple-element.25), channel_id=1, source_target_pairs={{1,0},{2,1},{3,2},{5,4},{6,5},{7,6},{9,8},{10,9},{11,10},{13,12},{... | collective-permute-start | bytes 196616 | tf_op jit(solution)/shard_map/ppermute | solution.py:17
  312.1 6.5 %collective-permute-start.4 = (f32[16,1024]{1,0:T(8,128)S(1)}, f32[16,1024]{1,0:T(8,128)S(1)}, u32[]{:S(2)}, u32[]{:S(2)}) collective-permute-start(f32[16,1024]{1,0:T(8,128)S(1)} %fusion.35), channel_id=1, source_target_pairs={{0,1},{1,2},{2,3},{4,5},{5,6},{6,7},{8,9},{9,10},{10,11},{12,13},{... | collective-permute-start | bytes 196616 | tf_op jit(solution)/shard_map/ppermute | solution.py:17
  325.6 12.7 %copy-start.2 = (bf16[1024,2048]{1,0:T(8,128)(2,1)S(1)}, bf16[1024,2048]{1,0:T(8,128)(2,1)}, u32[]{:S(2)}) copy-start(bf16[1024,2048]{1,0:T(8,128)(2,1)} %all-gather.2.cloned.1.call-done) | copy-start | bytes 12582916
  325.7 12.5 %collective-permute-start.5 = (f32[16,1024]{1,0:T(8,128)S(1)}, f32[16,1024]{1,0:T(8,128)S(1)}, u32[]{:S(2)}, u32[]{:S(2)}) collective-permute-start(f32[16,1024]{1,0:T(8,128)S(1)} %get-tuple-element.20), channel_id=1, source_target_pairs={{1,0},{2,1},{3,2},{5,4},{6,5},{7,6},{9,8},{10,9},{11,10},{13,12},{... | collective-permute-start | bytes 196616 | tf_op jit(solution)/shard_map/ppermute | solution.py:17
  331.7 6.5 %collective-permute-start.6 = (f32[16,1024]{1,0:T(8,128)S(1)}, f32[16,1024]{1,0:T(8,128)S(1)}, u32[]{:S(2)}, u32[]{:S(2)}) collective-permute-start(f32[16,1024]{1,0:T(8,128)S(1)} %fusion.32), channel_id=1, source_target_pairs={{0,1},{1,2},{2,3},{4,5},{5,6},{6,7},{8,9},{9,10},{10,11},{12,13},{... | collective-permute-start | bytes 196616 | tf_op jit(solution)/shard_map/ppermute | solution.py:17
  345.2 12.8 %copy-start.3 = (bf16[1024,2048]{1,0:T(8,128)(2,1)S(1)}, bf16[1024,2048]{1,0:T(8,128)(2,1)}, u32[]{:S(2)}) copy-start(bf16[1024,2048]{1,0:T(8,128)(2,1)} %all-gather.2.cloned.1.call-done) | copy-start | bytes 12582916
  346.0 12.1 %collective-permute-start.7 = (f32[16,1024]{1,0:T(8,128)S(1)}, f32[16,1024]{1,0:T(8,128)S(1)}, u32[]{:S(2)}, u32[]{:S(2)}) collective-permute-start(f32[16,1024]{1,0:T(8,128)S(1)} %get-tuple-element.16), channel_id=1, source_target_pairs={{1,0},{2,1},{3,2},{5,4},{6,5},{7,6},{9,8},{10,9},{11,10},{13,12},{... | collective-permute-start | bytes 196616 | tf_op jit(solution)/shard_map/ppermute | solution.py:17
  351.7 6.4 %collective-permute-start.8 = (f32[16,1024]{1,0:T(8,128)S(1)}, f32[16,1024]{1,0:T(8,128)S(1)}, u32[]{:S(2)}, u32[]{:S(2)}) collective-permute-start(f32[16,1024]{1,0:T(8,128)S(1)} %fusion.29), channel_id=1, source_target_pairs={{0,1},{1,2},{2,3},{4,5},{5,6},{6,7},{8,9},{9,10},{10,11},{12,13},{... | collective-permute-start | bytes 196616 | tf_op jit(solution)/shard_map/ppermute | solution.py:17
Sparse Core Ops, SparseCore 0:
  70.1 144.6 reduce-scatter.1
  217.2 71.1 all-gather.1
where the time goes:
time: 368 us; the launch traced here: 367 us
  waiting for transfers between devices  238 us (65%)
  matrix products  38.4 us (10%)
  blocking collectives  34.4 us (9%)
  starting transfers between devices  32.9 us (9%)
  between operations  14.3 us (4%)
  other arithmetic  8.78 us (2%)
    reduce_scatter x1, waiting for transfers between devices, on_device(): lax.psum_scatter(contract_rows(standard, joined), 'samples', scatter_dime...  145 us
    all_gather x1, waiting for transfers between devices, on_device(): gathered = lax.all_gather(link_rows, 'samples', axis=0, tiled=True)  68.8 us
    ppermute x9, starting transfers between devices, passed_along(): return lax.ppermute(block, axis, route)  32.8 us
    ppermute x9, waiting for transfers between devices, passed_along(): return lax.ppermute(block, axis, route)  24.8 us
    dot_general x8, matrix products, times_transpose(): lax.dot_general(vector, matrix, (((1,), (1,)), ((), ())), precision=HIGHE...  21.2 us
    psum x1, blocking collectives, on_device(): lax.psum((jnp.sum(dosage, axis=0), jnp.sum(dosage * dosage, axis=0)), 'sa...  19 us
    psum x3, blocking collectives, pair_sums(): lax.psum((local_sums(vector, vector), local_sums(vector, image)), 'vblocks')  15.4 us
    dot_general x4, matrix products, apply_link(): jnp.dot(vector, edge_block, precision=HIGHEST, preferred_element_type=jnp...  10.2 us
  transfers between devices with their start and end apart: 11, of which 3 were waited for; matrix products, arithmetic and copies ran while one was open for 6% of the time, Pallas kernels for 0%

commit v1 on v0

v1 whole, which is shorter than its diff:
```python
import functools

import jax
import jax.numpy as jnp
from jax import lax
from jax.experimental import pallas as pl
from jax.experimental.pallas import tpu as pltpu
from jax.sharding import PartitionSpec as P

ITERS = 3
RIDGE = 0.1
EPSILON = 1e-05
MESH = pl.DeviceIdType.MESH
ROWS = 256
TRAITS = 128
LANES = 128


def loop(count, body):
    if count <= 4:
        for index in range(count):
            body(index)
    else:
        lax.fori_loop(0, count, lambda index, carry: (body(index), carry)[1], 0)


def split_high_low(value):
    high = value.astype(jnp.bfloat16)
    low = (value - high.astype(jnp.float32)).astype(jnp.bfloat16)
    return jnp.concatenate([high, low], axis=0)


def kernel(
    n,
    nv,
    g_hbm,
    mask_ref,
    z_ref,
    sol_ref,
    imp_ref,
    g_buf,
    x_ref,
    stat,
    u_all,
    t_own,
    t_side,
    p_acc,
    p_send,
    p_recv,
    dots,
    g_sem,
    stat_ss,
    stat_rs,
    u_ss,
    u_rs,
    t_ss,
    t_rs,
    p_ss,
    p_rs,
    dot_ss,
    dot_rs,
):
    me = lax.axis_index("samples")
    mv = lax.axis_index("vblocks")
    tiles, _, width = g_buf.shape
    kd = z_ref.shape[0]
    chunks = (n * kd) // TRAITS
    per_chunk = TRAITS // kd
    packs = width // LANES
    total_samples = float(n * tiles * ROWS)

    for c in range(tiles):
        pltpu.make_async_copy(
            g_hbm.at[pl.ds(c * ROWS, ROWS)], g_buf.at[c], g_sem.at[c]
        ).start()

    barrier = pltpu.get_barrier_semaphore()

    def greet_samples(i):
        peer = lax.rem(me + i + 1, n)
        pl.semaphore_signal(barrier, inc=1, device_id=(peer, mv), device_id_type=MESH)

    def greet_blocks(i):
        peer = lax.rem(mv + i + 1, nv)
        pl.semaphore_signal(barrier, inc=1, device_id=(me, peer), device_id_type=MESH)

    loop(n - 1, greet_samples)
    loop(nv - 1, greet_blocks)

    def to_peer(buf, ss, rs, peer):
        return pltpu.make_async_remote_copy(
            src_ref=buf.at[me],
            dst_ref=buf.at[me],
            send_sem=ss.at[peer],
            recv_sem=rs.at[me],
            device_id=(peer, mv),
            device_id_type=MESH,
        )

    def from_peer(buf, ss, rs, peer):
        return pltpu.make_async_remote_copy(
            src_ref=buf.at[peer],
            dst_ref=buf.at[peer],
            send_sem=ss.at[peer],
            recv_sem=rs.at[peer],
            device_id=(peer, mv),
            device_id_type=MESH,
        )

    def each_peer(action):
        loop(n - 1, lambda i: action(lax.rem(me + i + 1, n)))

    totals = jnp.zeros((1, width), jnp.float32)
    squares = jnp.zeros((1, width), jnp.float32)
    for c in range(tiles):
        pltpu.make_async_copy(
            g_hbm.at[pl.ds(c * ROWS, ROWS)], g_buf.at[c], g_sem.at[c]
        ).wait()
        dosage = g_buf[c].astype(jnp.float32)
        totals = totals + jnp.sum(dosage, axis=0, keepdims=True)
        squares = squares + jnp.sum(dosage * dosage, axis=0, keepdims=True)
    for i in range(packs):
        stat[me, i : i + 1, :] = totals[:, i * LANES : (i + 1) * LANES]
        stat[me, packs + i : packs + i + 1, :] = squares[:, i * LANES : (i + 1) * LANES]
    mask_row = mask_ref[...].astype(jnp.float32)
    residual = mask_row * z_ref[...]
    u_all[me] = residual

    pl.semaphore_wait(barrier, n - 1 + nv - 1)
    each_peer(lambda q: to_peer(stat, stat_ss, stat_rs, q).start())
    each_peer(lambda q: to_peer(u_all, u_ss.at[0], u_rs.at[0], q).start())
    each_peer(lambda q: from_peer(stat, stat_ss, stat_rs, q).wait_recv())
    summed = jnp.sum(stat[...], axis=0)
    totals = jnp.concatenate([summed[i : i + 1] for i in range(packs)], axis=1)
    squares = jnp.concatenate([summed[packs + i : packs + i + 1] for i in range(packs)], axis=1)
    mean_dosage = totals / total_samples
    variance = squares / total_samples - mean_dosage * mean_dosage
    scale = lax.rsqrt(variance + EPSILON)
    for c in range(tiles):
        dosage = g_buf[c].astype(jnp.float32)
        x_ref[c] = ((dosage - mean_dosage) * scale).astype(jnp.bfloat16)
    each_peer(lambda q: to_peer(stat, stat_ss, stat_rs, q).wait_send())

    def t_copy(k, j, ahead):
        side = 0 if ahead else 1
        return pltpu.make_async_remote_copy(
            src_ref=t_own.at[j],
            dst_ref=t_side.at[side, j],
            send_sem=t_ss.at[k, side, j],
            recv_sem=t_rs.at[k, side, j],
            device_id=(me, mv + 1 if ahead else mv - 1),
            device_id_type=MESH,
        )

    @pl.when(mv == 0)
    def _():
        t_side[0] = jnp.zeros(t_side.shape[1:], t_side.dtype)

    @pl.when(mv == nv - 1)
    def _():
        t_side[1] = jnp.zeros(t_side.shape[1:], t_side.dtype)

    lane = lax.broadcasted_iota(jnp.int32, (kd, LANES), 1)

    def row_sums(first, second):
        return jnp.sum(first * second, axis=1, keepdims=True)

    direction = residual
    weights = jnp.zeros_like(residual)
    projected = jnp.zeros_like(residual)
    for k in range(ITERS):
        each_peer(lambda q: from_peer(u_all, u_ss.at[k], u_rs.at[k], q).wait_recv())

        def products(j):
            def one(c):
                u = u_all[pl.ds(c * per_chunk, per_chunk)].reshape(TRAITS, width)
                both = lax.dot_general(
                    split_high_low(u),
                    x_ref[j],
                    (((1,), (1,)), ((), ())),
                    preferred_element_type=jnp.float32,
                )
                t_own[j, pl.ds(pl.multiple_of(c * TRAITS, TRAITS), TRAITS)] = (
                    both[:TRAITS] + both[TRAITS:]
                ).astype(jnp.bfloat16)

            loop(chunks, one)

            @pl.when(mv < nv - 1)
            def _():
                t_copy(k, j, True).start()

            @pl.when(mv > 0)
            def _():
                t_copy(k, j, False).start()

        loop(tiles, products)

        def back(j):
            @pl.when(mv > 0)
            def _():
                t_copy(k, j, True).wait_recv()

            @pl.when(mv < nv - 1)
            def _():
                t_copy(k, j, False).wait_recv()

            def one(c):
                at = pl.ds(pl.multiple_of(c * TRAITS, TRAITS), TRAITS)
                mixed = t_own[j, at].astype(jnp.float32) + 0.5 * (
                    t_side[0, j, at].astype(jnp.float32) + t_side[1, j, at].astype(jnp.float32)
                )
                part = jnp.dot(
                    mixed.astype(jnp.bfloat16), x_ref[j], preferred_element_type=jnp.float32
                )
                if isinstance(j, int) and j == 0:
                    p_acc[at] = part
                else:
                    p_acc[at] = p_acc[at] + part

            loop(chunks, one)

        if tiles > 4:
            p_acc[...] = jnp.zeros_like(p_acc)
        loop(tiles, back)

        def to_send(c):
            at = pl.ds(pl.multiple_of(c * TRAITS, TRAITS), TRAITS)
            p_send[pl.ds(c * per_chunk, per_chunk)] = (
                (p_acc[at] * (1.0 / total_samples))
                .astype(jnp.bfloat16)
                .reshape(per_chunk, kd, width)
            )

        loop(chunks, to_send)

        def p_copy(q):
            return pltpu.make_async_remote_copy(
                src_ref=p_send.at[q],
                dst_ref=p_recv.at[me],
                send_sem=p_ss.at[k, q],
                recv_sem=p_rs.at[k, me],
                device_id=(q, mv),
                device_id_type=MESH,
            )

        each_peer(lambda q: p_copy(q).start())
        p_recv[me] = p_send[me]

        each_peer(lambda q: to_peer(u_all, u_ss.at[k], u_rs.at[k], q).wait_send())

        def t_sent(j):
            @pl.when(mv < nv - 1)
            def _():
                t_copy(k, j, True).wait_send()

            @pl.when(mv > 0)
            def _():
                t_copy(k, j, False).wait_send()

        loop(tiles, t_sent)
        each_peer(lambda q: from_peer(p_recv, p_ss.at[k], p_rs.at[k], q).wait_recv())
        linked = jnp.sum(p_recv[...].astype(jnp.float32), axis=0)
        each_peer(lambda q: p_copy(q).wait_send())

        image = mask_row * linked + RIDGE * direction
        parts = (
            row_sums(residual, residual),
            row_sums(direction, image),
            row_sums(residual, image),
            row_sums(image, image),
        )
        packed = jnp.zeros((kd, LANES), jnp.float32)
        for i, part in enumerate(parts):
            packed = jnp.where(lane == i, part, packed)
        dots[k, mv] = packed

        def dot_copy(slot, peer):
            return pltpu.make_async_remote_copy(
                src_ref=dots.at[k, slot],
                dst_ref=dots.at[k, slot],
                send_sem=dot_ss.at[k, peer],
                recv_sem=dot_rs.at[k, slot],
                device_id=(me, peer),
                device_id_type=MESH,
            )

        def each_block(action):
            loop(nv - 1, lambda i: action(lax.rem(mv + i + 1, nv)))

        each_block(lambda q: dot_copy(mv, q).start())
        each_block(lambda q: dot_copy(q, q).wait_recv())
        all_sums = jnp.sum(dots[k], axis=0)
        norm, product, cross, image_norm = [all_sums[:, i : i + 1] for i in range(4)]
        step = norm / product
        weights = weights + step * direction
        projected = projected + step * linked
        if k + 1 < ITERS:
            residual = residual - step * image
            norm_next = norm - 2.0 * step * cross + step * step * image_norm
            direction = residual + (norm_next / norm) * direction
            u_all[me] = direction
            each_peer(lambda q: to_peer(u_all, u_ss.at[k + 1], u_rs.at[k + 1], q).start())
        each_block(lambda q: dot_copy(mv, q).wait_send())

    sol_ref[...] = weights
    imp_ref[...] = jnp.where(mask_ref[...] == 1, z_ref[...], projected)


def on_device(genotypes, typed_mask, z_scores):
    n, nv = lax.axis_size("samples"), lax.axis_size("vblocks")
    samples_dev, width = genotypes.shape
    kd = z_scores.shape[0]
    traits = n * kd
    tiles = samples_dev // ROWS
    vmem = pl.BlockSpec(memory_space=pltpu.VMEM)
    dma = pltpu.SemaphoreType.DMA
    out = jax.ShapeDtypeStruct((kd, width), jnp.float32)
    return pl.pallas_call(
        functools.partial(kernel, n, nv),
        out_shape=(out, out),
        in_specs=[pl.BlockSpec(memory_space=pl.ANY), vmem, vmem],
        out_specs=(vmem, vmem),
        scratch_shapes=[
            pltpu.VMEM((tiles, ROWS, width), jnp.int32),
            pltpu.VMEM((tiles, ROWS, width), jnp.bfloat16),
            pltpu.VMEM((n, 2 * width // LANES, LANES), jnp.float32),
            pltpu.VMEM((n, kd, width), jnp.float32),
            pltpu.VMEM((tiles, traits, ROWS), jnp.bfloat16),
            pltpu.VMEM((2, tiles, traits, ROWS), jnp.bfloat16),
            pltpu.VMEM((traits, width), jnp.float32),
            pltpu.VMEM((n, kd, width), jnp.bfloat16),
            pltpu.VMEM((n, kd, width), jnp.bfloat16),
            pltpu.VMEM((ITERS, nv, kd, LANES), jnp.float32),
            dma((tiles,)),
            dma((n,)),
            dma((n,)),
            dma((ITERS, n)),
            dma((ITERS, n)),
            dma((ITERS, 2, tiles)),
            dma((ITERS, 2, tiles)),
            dma((ITERS, n)),
            dma((ITERS, n)),
            dma((ITERS, nv)),
            dma((ITERS, nv)),
        ],
        compiler_params=pltpu.CompilerParams(
            collective_id=0, has_side_effects=True, vmem_limit_bytes=56 << 20
        ),
    )(genotypes, typed_mask[None, :], z_scores)


def solution(mesh):
    placed = (P("samples", "vblocks"), P("vblocks"), P("samples", "vblocks"))
    return jax.shard_map(
        on_device,
        mesh=mesh,
        in_specs=placed,
        out_specs=(P("samples", "vblocks"), P("samples", "vblocks")),
        check_vma=False,
    )
```

time: 368 us -> 93.3 us (0.25)
  waiting for transfers between devices: 238 us -> 0 us
  Pallas kernels: 0 us -> 89.1 us
  matrix products: 38.4 us -> 0 us
  blocking collectives: 34.4 us -> 0 us
  starting transfers between devices: 32.9 us -> 0 us
  between operations: 14.3 us -> 0.64 us
  other arithmetic: 8.78 us -> 0 us
    reduce_scatter x1 -> x0, waiting for transfers between devices: 145 us -> none  [on_device(): lax.psum_scatter(contract_rows(standard, joined), 'samples', scatter_dime...]
    pallas_call x0 -> x1, Pallas kernels: none -> 89.1 us  [on_device(): pl.pallas_call(functools.partial(kernel, n, nv), out_shape=(out, out), in...]
    all_gather x1 -> x0, waiting for transfers between devices: 68.8 us -> none  [on_device(): gathered = lax.all_gather(link_rows, 'samples', axis=0, tiled=True)]
    dot_general x13 -> x0, matrix products: 38.4 us -> none  [the longest x8 21.2 us: times_transpose(): lax.dot_general(vector, matrix, (((1,), (1,)), ((), ())), precision=HIGHE...]
    psum x4 -> x0, blocking collectives: 34.4 us -> none  [the longest x1 19 us: on_device(): lax.psum((jnp.sum(dosage, axis=0), jnp.sum(dosage * dosage, axis=0)), 'sa...]
    ppermute x9 -> x0, starting transfers between devices: 32.8 us -> none  [passed_along(): return lax.ppermute(block, axis, route)]
    ppermute x9 -> x0, waiting for transfers between devices: 24.8 us -> none  [passed_along(): return lax.ppermute(block, axis, route)]
    convert_element_type x3 -> x0, other arithmetic: 4.91 us -> none  [the longest x1 2.81 us: on_device(): ((dosage - mean_dosage) * lax.rsqrt(variance + EPSILON)).astype(jnp.bfloa...]
  transfers between devices with their start and end apart: 11 -> 0, of which waited for: 3 -> 0; matrix products, arithmetic and copies ran while one was open for 6% -> 0% of each run, Pallas kernels for 0% -> 0%
where the time goes in v1:
time: 93.3 us; the launch traced here: 92.7 us
  Pallas kernels  89.1 us (95%)
  local copies, waits for them, and re-layouts  2.95 us (3%)
    pallas_call x1, Pallas kernels, on_device(): pl.pallas_call(functools.partial(kernel, n, nv), out_shape=(out, out), in...  89.1 us
    unnamed x2, local copies, waits for them, and re-layouts  2.95 us

profile of v1, /device:TPU:1, one launch (start us, length us, event | category | flops | bytes accessed | tf_op | source)
XLA Modules:
  0.0 92.7 jit_solution(13958016800733683908)
XLA Ops:
  0.6 89.1 %shard_map.50 = (f32[16,1024]{1,0:T(8,128)}, f32[16,1024]{1,0:T(8,128)}) custom-call(s32[1024,1024]{1,0:T(8,128)} %g_hbm.1, s32[1,1024]{1,0:T(1,128)} %bitcast.1, f32[16,1024]{1,0:T(8,128)} %z_ref.1), custom_call_target="tpu_custom_call" | custom-call | tf_op jit(solution)/shard_map/pallas_call | solution.py:319
  89.7 1.5 %copy.7 = f32[16,1024]{1,0:T(8,128)} copy(f32[16,1024]{1,0:T(8,128)} %get-tuple-element.4) | data formatting | bytes 131072
  91.2 1.5 %copy.8 = f32[16,1024]{1,0:T(8,128)} copy(f32[16,1024]{1,0:T(8,128)} %get-tuple-element.5) | data formatting | bytes 131072

commit v2 on v1

--- a/solution.py
+++ b/solution.py
@@ -28,6 +28,27 @@
     high = value.astype(jnp.bfloat16)
     low = (value - high.astype(jnp.float32)).astype(jnp.bfloat16)
     return jnp.concatenate([high, low], axis=0)
+
+
+LEVELS = 32000.0
+
+
+def decoded_scale(digits):
+    return digits[:, 0:1] * jnp.exp2(digits[:, 1:2] - 13.0)
+
+
+def encode(value):
+    rows = value.shape[0]
+    biggest = jnp.max(jnp.abs(value), axis=1, keepdims=True)
+    wanted = jnp.maximum(biggest, 1e-30) * (1.0 / LEVELS)
+    exponent = jnp.floor(jnp.log2(wanted))
+    mantissa = jnp.ceil(wanted * jnp.exp2(13.0 - exponent))
+    lane = lax.broadcasted_iota(jnp.int32, (rows, LANES), 1)
+    digits = jnp.where(lane == 0, mantissa, jnp.where(lane == 1, exponent, 0.0))
+    scale = decoded_scale(digits)
+    coded = jnp.round(value / scale)
+    both = jnp.concatenate([coded, digits], axis=1).astype(jnp.int32).astype(jnp.int16)
+    return both, coded * scale
 
 
 def kernel(
@@ -46,6 +67,7 @@
     t_side,
     p_acc,
     p_send,
+    p_pair,
     p_recv,
     dots,
     g_sem,
@@ -55,6 +77,8 @@
     u_rs,
     t_ss,
     t_rs,
+    pair_ss,
+    pair_rs,
     p_ss,
     p_rs,
     dot_ss,
@@ -109,6 +133,50 @@
 
     def each_peer(action):
         loop(n - 1, lambda i: action(lax.rem(me + i + 1, n)))
+
+    mine, parity = me // 2, lax.rem(me, 2)
+    partner = me + 1 - 2 * parity
+    pairs = n // 2
+
+    def each_far(action):
+        loop(pairs - 1, lambda i: action(lax.rem(mine + i + 1, pairs)))
+
+    def far_copy(k, slot, target):
+        return pltpu.make_async_remote_copy(
+            src_ref=u_all.at[slot],
+            dst_ref=u_all.at[slot],
+            send_sem=u_ss.at[k, 0, target // 2],
+            recv_sem=u_rs.at[k, slot],
+            device_id=(target, mv),
+            device_id_type=MESH,
+        )
+
+    def partner_copy(k, slot):
+        return pltpu.make_async_remote_copy(
+            src_ref=u_all.at[slot],
+            dst_ref=u_all.at[slot],
+            send_sem=u_ss.at[k, 1, slot // 2],
+            recv_sem=u_rs.at[k, slot],
+            device_id=(partner, mv),
+            device_id_type=MESH,
+        )
+
+    def start_gather(k):
+        each_far(lambda f: far_copy(k, me, 2 * f + parity).start())
+        partner_copy(k, me).start()
+
+    def end_gather(k):
+        def forward(f):
+            slot = 2 * f + parity
+            far_copy(k, slot, slot).wait_recv()
+            partner_copy(k, slot).start()
+
+        each_far(forward)
+        loop(pairs, lambda f: partner_copy(k, 2 * f + 1 - parity).wait_recv())
+
+    def gather_sent(k):
+        each_far(lambda f: far_copy(k, me, 2 * f + parity).wait_send())
+        loop(pairs, lambda f: partner_copy(k, 2 * f + parity).wait_send())
 
     totals = jnp.zeros((1, width), jnp.float32)
     squares = jnp.zeros((1, width), jnp.float32)
@@ -124,11 +192,11 @@
         stat[me, packs + i : packs + i + 1, :] = squares[:, i * LANES : (i + 1) * LANES]
     mask_row = mask_ref[...].astype(jnp.float32)
     residual = mask_row * z_ref[...]
-    u_all[me] = residual
+    u_all[me], direction = encode(residual)
 
     pl.semaphore_wait(barrier, n - 1 + nv - 1)
     each_peer(lambda q: to_peer(stat, stat_ss, stat_rs, q).start())
-    each_peer(lambda q: to_peer(u_all, u_ss.at[0], u_rs.at[0], q).start())
+    start_gather(0)
     each_peer(lambda q: from_peer(stat, stat_ss, stat_rs, q).wait_recv())
     summed = jnp.sum(stat[...], axis=0)
     totals = jnp.concatenate([summed[i : i + 1] for i in range(packs)], axis=1)
@@ -165,23 +233,23 @@
     def row_sums(first, second):
         return jnp.sum(first * second, axis=1, keepdims=True)
 
-    direction = residual
     weights = jnp.zeros_like(residual)
     projected = jnp.zeros_like(residual)
     for k in range(ITERS):
-        each_peer(lambda q: from_peer(u_all, u_ss.at[k], u_rs.at[k], q).wait_recv())
+        end_gather(k)
 
         def products(j):
             def one(c):
-                u = u_all[pl.ds(c * per_chunk, per_chunk)].reshape(TRAITS, width)
+                coded = u_all[pl.ds(c * per_chunk, per_chunk)].astype(jnp.int32)
+                coded = coded.astype(jnp.float32).reshape(TRAITS, width + LANES)
                 both = lax.dot_general(
-                    split_high_low(u),
+                    split_high_low(coded[:, :width]),
                     x_ref[j],
                     (((1,), (1,)), ((), ())),
                     preferred_element_type=jnp.float32,
                 )
                 t_own[j, pl.ds(pl.multiple_of(c * TRAITS, TRAITS), TRAITS)] = (
-                    both[:TRAITS] + both[TRAITS:]
+                    (both[:TRAITS] + both[TRAITS:]) * decoded_scale(coded[:, width:])
                 ).astype(jnp.bfloat16)
 
             loop(chunks, one)
@@ -234,20 +302,45 @@
 
         loop(chunks, to_send)
 
-        def p_copy(q):
+        def pair_copy(f, own):
+            slot = 2 * f + (parity if own else 1 - parity)
             return pltpu.make_async_remote_copy(
-                src_ref=p_send.at[q],
-                dst_ref=p_recv.at[me],
-                send_sem=p_ss.at[k, q],
-                recv_sem=p_rs.at[k, me],
-                device_id=(q, mv),
+                src_ref=p_send.at[slot],
+                dst_ref=p_pair.at[f],
+                send_sem=pair_ss.at[k, f],
+                recv_sem=pair_rs.at[k, f],
+                device_id=(partner, mv),
                 device_id_type=MESH,
             )
 
-        each_peer(lambda q: p_copy(q).start())
-        p_recv[me] = p_send[me]
-
-        each_peer(lambda q: to_peer(u_all, u_ss.at[k], u_rs.at[k], q).wait_send())
+        def p_copy(f, slot):
+            return pltpu.make_async_remote_copy(
+                src_ref=p_send.at[2 * f + parity],
+                dst_ref=p_recv.at[slot],
+                send_sem=p_ss.at[k, f],
+                recv_sem=p_rs.at[k, slot],
+                device_id=(2 * f + parity, mv),
+                device_id_type=MESH,
+            )
+
+        def add_pair(f):
+            pair_copy(f, True).wait_recv()
+            slot = 2 * f + parity
+            p_send[slot] = (
+                p_send[slot].astype(jnp.float32) + p_pair[f].astype(jnp.float32)
+            ).astype(jnp.bfloat16)
+
+        def add_and_send(f):
+            add_pair(f)
+            p_copy(f, mine).start()
+
+        gather_sent(k)
+        each_far(lambda f: pair_copy(f, False).start())
+        pair_copy(mine, False).start()
+        each_far(add_and_send)
+        add_pair(mine)
+        p_recv[mine] = p_send[me]
+
 
         def t_sent(j):
             @pl.when(mv < nv - 1)
@@ -259,9 +352,10 @@
                 t_copy(k, j, False).wait_send()
 
         loop(tiles, t_sent)
-        each_peer(lambda q: from_peer(p_recv, p_ss.at[k], p_rs.at[k], q).wait_recv())
+        each_far(lambda f: p_copy(f, f).wait_recv())
         linked = jnp.sum(p_recv[...].astype(jnp.float32), axis=0)
-        each_peer(lambda q: p_copy(q).wait_send())
+        loop(pairs, lambda f: pair_copy(f, False).wait_send())
+        each_far(lambda f: p_copy(f, mine).wait_send())
 
         image = mask_row * linked + RIDGE * direction
         parts = (
@@ -299,8 +393,8 @@
             residual = residual - step * image
             norm_next = norm - 2.0 * step * cross + step * step * image_norm
             direction = residual + (norm_next / norm) * direction
-            u_all[me] = direction
-            each_peer(lambda q: to_peer(u_all, u_ss.at[k + 1], u_rs.at[k + 1], q).start())
+            u_all[me], direction = encode(direction)
+            start_gather(k + 1)
         each_block(lambda q: dot_copy(mv, q).wait_send())
 
     sol_ref[...] = weights
@@ -325,22 +419,25 @@
             pltpu.VMEM((tiles, ROWS, width), jnp.int32),
             pltpu.VMEM((tiles, ROWS, width), jnp.bfloat16),
             pltpu.VMEM((n, 2 * width // LANES, LANES), jnp.float32),
-            pltpu.VMEM((n, kd, width), jnp.float32),
+            pltpu.VMEM((n, kd, width + LANES), jnp.int16),
             pltpu.VMEM((tiles, traits, ROWS), jnp.bfloat16),
             pltpu.VMEM((2, tiles, traits, ROWS), jnp.bfloat16),
             pltpu.VMEM((traits, width), jnp.float32),
             pltpu.VMEM((n, kd, width), jnp.bfloat16),
-            pltpu.VMEM((n, kd, width), jnp.bfloat16),
+            pltpu.VMEM((n // 2, kd, width), jnp.bfloat16),
+            pltpu.VMEM((n // 2, kd, width), jnp.bfloat16),
             pltpu.VMEM((ITERS, nv, kd, LANES), jnp.float32),
             dma((tiles,)),
             dma((n,)),
             dma((n,)),
-            dma((ITERS, n)),
+            dma((ITERS, 2, n // 2)),
             dma((ITERS, n)),
             dma((ITERS, 2, tiles)),
             dma((ITERS, 2, tiles)),
-            dma((ITERS, n)),
-            dma((ITERS, n)),
+            dma((ITERS, n // 2)),
+            dma((ITERS, n // 2)),
+            dma((ITERS, n // 2)),
+            dma((ITERS, n // 2)),
             dma((ITERS, nv)),
             dma((ITERS, nv)),
         ],

time: 93.3 us -> 82.8 us (0.89)
  Pallas kernels: 89.1 us -> 78.6 us
    pallas_call x1, Pallas kernels: 89.1 us -> 78.6 us  [on_device(): pl.pallas_call(functools.partial(kernel, n, nv), out_shape=(out, out), in...]
where the time goes in v2:
time: 82.8 us; the launch traced here: 82.2 us
  Pallas kernels  78.6 us (95%)
  local copies, waits for them, and re-layouts  2.95 us (4%)
    pallas_call x1, Pallas kernels, on_device(): pl.pallas_call(functools.partial(kernel, n, nv), out_shape=(out, out), in...  78.6 us
    unnamed x2, local copies, waits for them, and re-layouts  2.95 us

profile of v2, /device:TPU:1, one launch (start us, length us, event | category | flops | bytes accessed | tf_op | source)
XLA Modules:
  0.0 82.2 jit_solution(5692115441837149241)
XLA Ops:
  0.6 78.6 %shard_map.50 = (f32[16,1024]{1,0:T(8,128)}, f32[16,1024]{1,0:T(8,128)}) custom-call(s32[1024,1024]{1,0:T(8,128)} %g_hbm.1, s32[1,1024]{1,0:T(1,128)} %bitcast.1, f32[16,1024]{1,0:T(8,128)} %z_ref.1), custom_call_target="tpu_custom_call" | custom-call | tf_op jit(solution)/shard_map/pallas_call | solution.py:413
  79.2 1.5 %copy.7 = f32[16,1024]{1,0:T(8,128)} copy(f32[16,1024]{1,0:T(8,128)} %get-tuple-element.4) | data formatting | bytes 131072
  80.7 1.5 %copy.8 = f32[16,1024]{1,0:T(8,128)} copy(f32[16,1024]{1,0:T(8,128)} %get-tuple-element.5) | data formatting | bytes 131072

commit v3 on v2

v3 whole, which is shorter than its diff:
```python
import functools

import jax
import jax.numpy as jnp
from jax import lax
from jax.experimental import pallas as pl
from jax.experimental.pallas import tpu as pltpu
from jax.sharding import PartitionSpec as P

ITERS = 3
RIDGE = 0.1
EPSILON = 1e-05
MESH = pl.DeviceIdType.MESH
ROWS = 256
TRAITS = 128
GROUPS = 1
LANES = 128


def loop(count, body):
    if count <= 4:
        for index in range(count):
            body(index)
    else:
        lax.fori_loop(0, count, lambda index, carry: (body(index), carry)[1], 0)


def split_high_low(value):
    high = value.astype(jnp.bfloat16)
    low = (value - high.astype(jnp.float32)).astype(jnp.bfloat16)
    return jnp.concatenate([high, low], axis=0)


LEVELS = 32000.0


def decoded_scale(digits):
    return digits[:, 0:1] * jnp.exp2(digits[:, 1:2] - 13.0)


def encode(value):
    rows = value.shape[0]
    biggest = jnp.max(jnp.abs(value), axis=1, keepdims=True)
    wanted = jnp.maximum(biggest, 1e-30) * (1.0 / LEVELS)
    exponent = jnp.floor(jnp.log2(wanted))
    mantissa = jnp.ceil(wanted * jnp.exp2(13.0 - exponent))
    lane = lax.broadcasted_iota(jnp.int32, (rows, LANES), 1)
    digits = jnp.where(lane == 0, mantissa, jnp.where(lane == 1, exponent, 0.0))
    scale = decoded_scale(digits)
    coded = jnp.round(value / scale)
    both = jnp.concatenate([coded, digits], axis=1).astype(jnp.int32).astype(jnp.int16)
    return both, coded * scale


def kernel(
    n,
    nv,
    g_hbm,
    mask_ref,
    z_ref,
    sol_ref,
    imp_ref,
    g_buf,
    x_ref,
    xt_ref,
    stat,
    u_all,
    u_hl,
    u_scale,
    res_ref,
    dir_ref,
    link_ref,
    t_own,
    t_side,
    p_acc,
    p_send,
    p_pair,
    p_recv,
    dots,
    g_sem,
    stat_ss,
    stat_rs,
    u_ss,
    u_rs,
    t_ss,
    t_rs,
    pair_ss,
    pair_rs,
    p_ss,
    p_rs,
    dot_ss,
    dot_rs,
):
    me = lax.axis_index("samples")
    mv = lax.axis_index("vblocks")
    tiles, _, width = g_buf.shape
    kd = z_ref.shape[0]
    packs = width // LANES
    total_samples = float(n * tiles * ROWS)

    for c in range(tiles):
        pltpu.make_async_copy(
            g_hbm.at[pl.ds(c * ROWS, ROWS)], g_buf.at[c], g_sem.at[c]
        ).start()

    barrier = pltpu.get_barrier_semaphore()

    def greet_samples(i):
        peer = lax.rem(me + i + 1, n)
        pl.semaphore_signal(barrier, inc=1, device_id=(peer, mv), device_id_type=MESH)

    def greet_blocks(i):
        peer = lax.rem(mv + i + 1, nv)
        pl.semaphore_signal(barrier, inc=1, device_id=(me, peer), device_id_type=MESH)

    loop(n - 1, greet_samples)
    loop(nv - 1, greet_blocks)

    def to_peer(buf, ss, rs, peer):
        return pltpu.make_async_remote_copy(
            src_ref=buf.at[me],
            dst_ref=buf.at[me],
            send_sem=ss.at[peer],
            recv_sem=rs.at[me],
            device_id=(peer, mv),
            device_id_type=MESH,
        )

    def from_peer(buf, ss, rs, peer):
        return pltpu.make_async_remote_copy(
            src_ref=buf.at[peer],
            dst_ref=buf.at[peer],
            send_sem=ss.at[peer],
            recv_sem=rs.at[peer],
            device_id=(peer, mv),
            device_id_type=MESH,
        )

    def each_peer(action):
        loop(n - 1, lambda i: action(lax.rem(me + i + 1, n)))

    mine, parity = me // 2, lax.rem(me, 2)
    partner = me + 1 - 2 * parity
    pairs = n // 2
    my_group = lax.rem(mine, GROUPS)
    members = pairs // GROUPS

    def each_far(action):
        loop(pairs - 1, lambda i: action(lax.rem(mine + i + 1, pairs)))

    def each_member(g, action):
        start = mine // GROUPS + 1
        loop(members, lambda i: action(GROUPS * lax.rem(start + i, members) + g))

    def slot_of(ref, f, side):
        return ref.at[lax.rem(f, GROUPS), 2 * (f // GROUPS) + side]

    def far_copy(k, f, target):
        return pltpu.make_async_remote_copy(
            src_ref=slot_of(u_all, f, parity),
            dst_ref=slot_of(u_all, f, parity),
            send_sem=u_ss.at[k, 0, target],
            recv_sem=u_rs.at[k, 2 * f + parity],
            device_id=(2 * target + parity, mv),
            device_id_type=MESH,
        )

    def partner_copy(k, f, side):
        return pltpu.make_async_remote_copy(
            src_ref=slot_of(u_all, f, side),
            dst_ref=slot_of(u_all, f, side),
            send_sem=u_ss.at[k, 1, f],
            recv_sem=u_rs.at[k, 2 * f + side],
            device_id=(partner, mv),
            device_id_type=MESH,
        )

    def start_gather(k):
        each_far(lambda f: far_copy(k, mine, f).start())
        partner_copy(k, mine, parity).start()

    def end_gather(k, g):
        def forward(f):
            @pl.when(f != mine)
            def _():
                far_copy(k, f, f).wait_recv()
                partner_copy(k, f, parity).start()

        each_member(g, forward)
        each_member(g, lambda f: partner_copy(k, f, 1 - parity).wait_recv())

    def gather_sent(k, g):
        @pl.when(my_group == g)
        def _():
            each_far(lambda f: far_copy(k, mine, f).wait_send())

        each_member(g, lambda f: partner_copy(k, f, parity).wait_send())

    totals = jnp.zeros((1, width), jnp.float32)
    squares = jnp.zeros((1, width), jnp.float32)
    for c in range(tiles):
        pltpu.make_async_copy(
            g_hbm.at[pl.ds(c * ROWS, ROWS)], g_buf.at[c], g_sem.at[c]
        ).wait()
        dosage = g_buf[c].astype(jnp.float32)
        totals = totals + jnp.sum(dosage, axis=0, keepdims=True)
        squares = squares + jnp.sum(dosage * dosage, axis=0, keepdims=True)
    for i in range(packs):
        stat[me, i : i + 1, :] = totals[:, i * LANES : (i + 1) * LANES]
        stat[me, packs + i : packs + i + 1, :] = squares[:, i * LANES : (i + 1) * LANES]
    mask_row = mask_ref[...].astype(jnp.float32)
    residual = mask_row * z_ref[...]
    res_ref[...] = residual
    my_slot = slot_of(u_all, mine, parity)
    my_slot[...], dir_ref[...] = encode(residual)
    sol_ref[...] = jnp.zeros_like(residual)
    imp_ref[...] = jnp.zeros_like(residual)

    pl.semaphore_wait(barrier, n - 1 + nv - 1)
    each_peer(lambda q: to_peer(stat, stat_ss, stat_rs, q).start())
    start_gather(0)
    each_peer(lambda q: from_peer(stat, stat_ss, stat_rs, q).wait_recv())
    summed = jnp.sum(stat[...], axis=0)
    totals = jnp.concatenate([summed[i : i + 1] for i in range(packs)], axis=1)
    squares = jnp.concatenate([summed[packs + i : packs + i + 1] for i in range(packs)], axis=1)
    mean_dosage = totals / total_samples
    variance = squares / total_samples - mean_dosage * mean_dosage
    scale = lax.rsqrt(variance + EPSILON)
    for c in range(tiles):
        dosage = g_buf[c].astype(jnp.float32)
        x_ref[c] = ((dosage - mean_dosage) * scale).astype(jnp.bfloat16)
    each_peer(lambda q: to_peer(stat, stat_ss, stat_rs, q).wait_send())

    def t_copy(k, g, j, ahead):
        side = 0 if ahead else 1
        return pltpu.make_async_remote_copy(
            src_ref=t_own.at[g, j],
            dst_ref=t_side.at[g, side, j],
            send_sem=t_ss.at[k, g, side, j],
            recv_sem=t_rs.at[k, g, side, j],
            device_id=(me, mv + 1 if ahead else mv - 1),
            device_id_type=MESH,
        )

    @pl.when(mv == 0)
    def _():
        for g in range(GROUPS):
            t_side[g, 0] = jnp.zeros(t_side.shape[2:], t_side.dtype)

    @pl.when(mv == nv - 1)
    def _():
        for g in range(GROUPS):
            t_side[g, 1] = jnp.zeros(t_side.shape[2:], t_side.dtype)

    lane = lax.broadcasted_iota(jnp.int32, (kd, LANES), 1)

    def row_sums(first, second):
        return jnp.sum(first * second, axis=1, keepdims=True)

    traits = u_hl.shape[1] // 2
    chunks = u_hl.shape[0]
    per_chunk = traits // kd

    def rows_at(c):
        return pl.ds(pl.multiple_of(c * traits, traits), traits)

    def project(k, g):
        end_gather(k, g)

        def decode(c):
            coded = u_all[g, pl.ds(c * per_chunk, per_chunk)].astype(jnp.int32)
            coded = coded.astype(jnp.float32).reshape(traits, width + LANES)
            u_hl[c] = split_high_low(coded[:, :width])
            u_scale[c] = jnp.broadcast_to(decoded_scale(coded[:, width:]), (traits, LANES))

        loop(chunks, decode)

        def products(j):
            def one(c):
                if k == 0:
                    both = lax.dot_general(
                        u_hl[c],
                        x_ref[j],
                        (((1,), (1,)), ((), ())),
                        preferred_element_type=jnp.float32,
                    )
                else:
                    both = jnp.dot(u_hl[c], xt_ref[j], preferred_element_type=jnp.float32)
                t_own[g, j, rows_at(c)] = (
                    (both[:traits] + both[traits:]) * u_scale[c, :, 0:1]
                ).astype(jnp.bfloat16)

            loop(chunks, one)

            @pl.when(mv < nv - 1)
            def _():
                t_copy(k, g, j, True).start()

            @pl.when(mv > 0)
            def _():
                t_copy(k, g, j, False).start()

        loop(tiles, products)

    def pair_copy(k, f, side):
        return pltpu.make_async_remote_copy(
            src_ref=slot_of(p_send, f, side),
            dst_ref=p_pair.at[f],
            send_sem=pair_ss.at[k, f],
            recv_sem=pair_rs.at[k, f],
            device_id=(partner, mv),
            device_id_type=MESH,
        )

    def p_copy(k, f, place):
        return pltpu.make_async_remote_copy(
            src_ref=slot_of(p_send, f, parity),
            dst_ref=p_recv.at[place],
            send_sem=p_ss.at[k, f],
            recv_sem=p_rs.at[k, place],
            device_id=(2 * f + parity, mv),
            device_id_type=MESH,
        )

    def project_back(k, g):
        def back(j):
            @pl.when(mv > 0)
            def _():
                t_copy(k, g, j, True).wait_recv()

            @pl.when(mv < nv - 1)
            def _():
                t_copy(k, g, j, False).wait_recv()

            def one(c):
                at = rows_at(c)
                sides = t_side[g, 0, j, at].astype(jnp.float32) + t_side[g, 1, j, at].astype(
                    jnp.float32
                )
                mixed = t_own[g, j, at].astype(jnp.float32) + 0.5 * sides
                part = jnp.dot(
                    mixed.astype(jnp.bfloat16), x_ref[j], preferred_element_type=jnp.float32
                )
                if isinstance(j, int) and j == 0:
                    p_acc[at] = part
                else:
                    p_acc[at] = p_acc[at] + part

            loop(chunks, one)

        if tiles > 4:
            p_acc[...] = jnp.zeros_like(p_acc)
        loop(tiles, back)

        def to_send(c):
            p_send[g, pl.ds(c * per_chunk, per_chunk)] = (
                (p_acc[rows_at(c)] * (1.0 / total_samples))
                .astype(jnp.bfloat16)
                .reshape(per_chunk, kd, width)
            )

        loop(chunks, to_send)
        gather_sent(k, g)
        each_member(g, lambda f: pair_copy(k, f, 1 - parity).start())

        def t_sent(j):
            @pl.when(mv < nv - 1)
            def _():
                t_copy(k, g, j, True).wait_send()

            @pl.when(mv > 0)
            def _():
                t_copy(k, g, j, False).wait_send()

        loop(tiles, t_sent)

    def add_pairs(k, g):
        def add(f):
            pair_copy(k, f, parity).wait_recv()
            held = slot_of(p_send, f, parity)
            both = held[...].astype(jnp.float32) + p_pair[f].astype(jnp.float32)
            held[...] = both.astype(jnp.bfloat16)

            @pl.when(f != mine)
            def _():
                p_copy(k, f, mine).start()

            @pl.when(f == mine)
            def _():
                p_recv[mine] = held[...]

        each_member(g, add)

    def dot_copy(k, slot, peer):
        return pltpu.make_async_remote_copy(
            src_ref=dots.at[k, slot],
            dst_ref=dots.at[k, slot],
            send_sem=dot_ss.at[k, peer],
            recv_sem=dot_rs.at[k, slot],
            device_id=(me, peer),
            device_id_type=MESH,
        )

    def each_block(action):
        loop(nv - 1, lambda i: action(lax.rem(mv + i + 1, nv)))

    def send_dots(k):
        each_far(lambda f: p_copy(k, f, f).wait_recv())
        linked = jnp.sum(p_recv[...].astype(jnp.float32), axis=0)
        residual, direction = res_ref[...], dir_ref[...]
        image = mask_row * linked + RIDGE * direction
        link_ref[...] = linked
        parts = (
            row_sums(residual, residual),
            row_sums(direction, image),
            row_sums(residual, image),
            row_sums(image, image),
        )
        packed = jnp.zeros((kd, LANES), jnp.float32)
        for i, part in enumerate(parts):
            packed = jnp.where(lane == i, part, packed)
        dots[k, mv] = packed
        each_block(lambda q: dot_copy(k, mv, q).start())

    def update(k):
        each_block(lambda q: dot_copy(k, q, q).wait_recv())
        all_sums = jnp.sum(dots[k], axis=0)
        norm, product, cross, image_norm = [all_sums[:, i : i + 1] for i in range(4)]
        step = norm / product
        direction, linked = dir_ref[...], link_ref[...]
        if k + 1 < ITERS:
            image = mask_row * linked + RIDGE * direction
            residual = res_ref[...] - step * image
            norm_next = norm - 2.0 * step * cross + step * step * image_norm
            my_slot[...], dir_ref[...] = encode(residual + (norm_next / norm) * direction)
            start_gather(k + 1)
            res_ref[...] = residual
            sol_ref[...] = sol_ref[...] + step * direction
            imp_ref[...] = imp_ref[...] + step * linked
        else:
            sol_ref[...] = sol_ref[...] + step * direction
            projected = imp_ref[...] + step * linked
            imp_ref[...] = jnp.where(mask_ref[...] == 1, z_ref[...], projected)

    def finish(k, g):
        each_member(g, lambda f: pair_copy(k, f, 1 - parity).wait_send())

        def sent(f):
            @pl.when(f != mine)
            def _():
                p_copy(k, f, mine).wait_send()

        each_member(g, sent)

        @pl.when(my_group == g)
        def _():
            each_block(lambda q: dot_copy(k, mv, q).wait_send())

    def transpose(j):
        xt_ref[j] = x_ref[j].T

    groups = range(GROUPS)
    for k in range(ITERS):
        for g in groups:
            project(k, g)
        for g in groups:
            project_back(k, g)
        if k == 0:
            loop(tiles // 2, transpose)
        for g in groups:
            add_pairs(k, g)
        if k == 0:
            loop(tiles - tiles // 2, lambda j: transpose(tiles // 2 + j))
        for g in groups:
            pl.when(my_group == g)(functools.partial(send_dots, k))
        for g in groups:
            pl.when(my_group == g)(functools.partial(update, k))
        for g in groups:
            finish(k, g)


def on_device(genotypes, typed_mask, z_scores):
    n, nv = lax.axis_size("samples"), lax.axis_size("vblocks")
    samples_dev, width = genotypes.shape
    kd = z_scores.shape[0]
    group_traits = n * kd // GROUPS
    tiles = samples_dev // ROWS
    vmem = pl.BlockSpec(memory_space=pltpu.VMEM)
    dma = pltpu.SemaphoreType.DMA
    out = jax.ShapeDtypeStruct((kd, width), jnp.float32)
    return pl.pallas_call(
        functools.partial(kernel, n, nv),
        out_shape=(out, out),
        in_specs=[pl.BlockSpec(memory_space=pl.ANY), vmem, vmem],
        out_specs=(vmem, vmem),
        scratch_shapes=[
            pltpu.VMEM((tiles, ROWS, width), jnp.int32),
            pltpu.VMEM((tiles, ROWS, width), jnp.bfloat16),
            pltpu.VMEM((tiles, width, ROWS), jnp.bfloat16),
            pltpu.VMEM((n, 2 * width // LANES, LANES), jnp.float32),
            pltpu.VMEM((GROUPS, n // GROUPS, kd, width + LANES), jnp.int16),
            pltpu.VMEM((group_traits // TRAITS, 2 * TRAITS, width), jnp.bfloat16),
            pltpu.VMEM((group_traits // TRAITS, TRAITS, LANES), jnp.float32),
            pltpu.VMEM((kd, width), jnp.float32),
            pltpu.VMEM((kd, width), jnp.float32),
            pltpu.VMEM((kd, width), jnp.float32),
            pltpu.VMEM((GROUPS, tiles, group_traits, ROWS), jnp.bfloat16),
            pltpu.VMEM((GROUPS, 2, tiles, group_traits, ROWS), jnp.bfloat16),
            pltpu.VMEM((group_traits, width), jnp.float32),
            pltpu.VMEM((GROUPS, n // GROUPS, kd, width), jnp.bfloat16),
            pltpu.VMEM((n // 2, kd, width), jnp.bfloat16),
            pltpu.VMEM((n // 2, kd, width), jnp.bfloat16),
            pltpu.VMEM((ITERS, nv, kd, LANES), jnp.float32),
            dma((tiles,)),
            dma((n,)),
            dma((n,)),
            dma((ITERS, 2, n // 2)),
            dma((ITERS, n)),
            dma((ITERS, GROUPS, 2, tiles)),
            dma((ITERS, GROUPS, 2, tiles)),
            dma((ITERS, n // 2)),
            dma((ITERS, n // 2)),
            dma((ITERS, n // 2)),
            dma((ITERS, n // 2)),
            dma((ITERS, nv)),
            dma((ITERS, nv)),
        ],
        compiler_params=pltpu.CompilerParams(
            collective_id=0, has_side_effects=True, vmem_limit_bytes=56 << 20
        ),
    )(genotypes, typed_mask[None, :], z_scores)


def solution(mesh):
    placed = (P("samples", "vblocks"), P("vblocks"), P("samples", "vblocks"))
    return jax.shard_map(
        on_device,
        mesh=mesh,
        in_specs=placed,
        out_specs=(P("samples", "vblocks"), P("samples", "vblocks")),
        check_vma=False,
    )
```

time: 82.8 us -> 82.6 us (level)
  no operation moved by 1% of the time
where the time goes in v3:
time: 82.6 us; the launch traced here: 82.1 us
  Pallas kernels  78.5 us (95%)
  local copies, waits for them, and re-layouts  2.95 us (4%)
    pallas_call x1, Pallas kernels, on_device(): pl.pallas_call(functools.partial(kernel, n, nv), out_shape=(out, out), in...  78.5 us
    unnamed x2, local copies, waits for them, and re-layouts  2.95 us

profile of v3, /device:TPU:1, one launch (start us, length us, event | category | flops | bytes accessed | tf_op | source)
XLA Modules:
  0.0 82.1 jit_solution(12141394703237272614)
XLA Ops:
  0.6 78.5 %shard_map.50 = (f32[16,1024]{1,0:T(8,128)}, f32[16,1024]{1,0:T(8,128)}) custom-call(s32[1024,1024]{1,0:T(8,128)} %g_hbm.1, s32[1,1024]{1,0:T(1,128)} %bitcast.1, f32[16,1024]{1,0:T(8,128)} %z_ref.1), custom_call_target="tpu_custom_call" | custom-call | tf_op jit(solution)/shard_map/pallas_call | solution.py:491
  79.1 1.5 %copy.7 = f32[16,1024]{1,0:T(8,128)} copy(f32[16,1024]{1,0:T(8,128)} %get-tuple-element.4) | data formatting | bytes 131072
  80.6 1.5 %copy.8 = f32[16,1024]{1,0:T(8,128)} copy(f32[16,1024]{1,0:T(8,128)} %get-tuple-element.5) | data formatting | bytes 131072

commit v4 on v3

--- a/solution.py
+++ b/solution.py
@@ -41,15 +41,21 @@
 def encode(value):
     rows = value.shape[0]
     biggest = jnp.max(jnp.abs(value), axis=1, keepdims=True)
-    wanted = jnp.maximum(biggest, 1e-30) * (1.0 / LEVELS)
+    wanted = jnp.maximum(biggest, 1e-28) * (1.0 / LEVELS)
     exponent = jnp.floor(jnp.log2(wanted))
     mantissa = jnp.ceil(wanted * jnp.exp2(13.0 - exponent))
     lane = lax.broadcasted_iota(jnp.int32, (rows, LANES), 1)
     digits = jnp.where(lane == 0, mantissa, jnp.where(lane == 1, exponent, 0.0))
     scale = decoded_scale(digits)
-    coded = jnp.round(value / scale)
+    coded = jnp.round(value * (1.0 / scale))
     both = jnp.concatenate([coded, digits], axis=1).astype(jnp.int32).astype(jnp.int16)
     return both, coded * scale
+
+
+def decode_rows(both):
+    both = both.astype(jnp.int32).astype(jnp.float32)
+    width = both.shape[1] - LANES
+    return both[:, :width] * decoded_scale(both[:, width:])
 
 
 def kernel(
@@ -76,7 +82,9 @@
     p_send,
     p_pair,
     p_recv,
-    dots,
+    norms,
+    block_forms,
+    sample_forms,
     g_sem,
     stat_ss,
     stat_rs,
@@ -88,8 +96,12 @@
     pair_rs,
     p_ss,
     p_rs,
-    dot_ss,
-    dot_rs,
+    norm_ss,
+    norm_rs,
+    bf_ss,
+    bf_rs,
+    sf_ss,
+    sf_rs,
 ):
     me = lax.axis_index("samples")
     mv = lax.axis_index("vblocks")
@@ -210,9 +222,10 @@
         stat[me, packs + i : packs + i + 1, :] = squares[:, i * LANES : (i + 1) * LANES]
     mask_row = mask_ref[...].astype(jnp.float32)
     residual = mask_row * z_ref[...]
-    res_ref[...] = residual
     my_slot = slot_of(u_all, mine, parity)
-    my_slot[...], dir_ref[...] = encode(residual)
+    my_slot[...], res_ref[...] = encode(residual)
+    dir_ref[...] = jnp.zeros_like(residual)
+    link_ref[...] = jnp.zeros_like(residual)
     sol_ref[...] = jnp.zeros_like(residual)
     imp_ref[...] = jnp.zeros_like(residual)
 
@@ -252,8 +265,6 @@
         for g in range(GROUPS):
             t_side[g, 1] = jnp.zeros(t_side.shape[2:], t_side.dtype)
 
-    lane = lax.broadcasted_iota(jnp.int32, (kd, LANES), 1)
-
     def row_sums(first, second):
         return jnp.sum(first * second, axis=1, keepdims=True)
 
@@ -338,6 +349,17 @@
                     jnp.float32
                 )
                 mixed = t_own[g, j, at].astype(jnp.float32) + 0.5 * sides
+                forms = lax.dot_general(
+                    jnp.ones((8, ROWS), jnp.bfloat16),
+                    split_high_low(t_own[g, j, at].astype(jnp.float32) * mixed),
+                    (((1,), (1,)), ((), ())),
+                    preferred_element_type=jnp.float32,
+                )
+                form = forms[:, :traits] + forms[:, traits:]
+                if isinstance(j, int) and j == 0:
+                    block_forms[k, mv, c] = form
+                else:
+                    block_forms[k, mv, c] = block_forms[k, mv, c] + form
                 part = jnp.dot(
                     mixed.astype(jnp.bfloat16), x_ref[j], preferred_element_type=jnp.float32
                 )
@@ -350,18 +372,19 @@
 
         if tiles > 4:
             p_acc[...] = jnp.zeros_like(p_acc)
+            block_forms[k, mv] = jnp.zeros(block_forms.shape[2:], jnp.float32)
         loop(tiles, back)
 
         def to_send(c):
-            p_send[g, pl.ds(c * per_chunk, per_chunk)] = (
-                (p_acc[rows_at(c)] * (1.0 / total_samples))
-                .astype(jnp.bfloat16)
-                .reshape(per_chunk, kd, width)
+            pieces, _ = encode(p_acc[rows_at(c)] * (1.0 / total_samples))
+            p_send[g, pl.ds(c * per_chunk, per_chunk)] = pieces.reshape(
+                per_chunk, kd, width + LANES
             )
 
         loop(chunks, to_send)
         gather_sent(k, g)
         each_member(g, lambda f: pair_copy(k, f, 1 - parity).start())
+        each_block(lambda q: across_blocks(block_forms, bf_ss, bf_rs, k, mv, q).start())
 
         def t_sent(j):
             @pl.when(mv < nv - 1)
@@ -378,8 +401,7 @@
         def add(f):
             pair_copy(k, f, parity).wait_recv()
             held = slot_of(p_send, f, parity)
-            both = held[...].astype(jnp.float32) + p_pair[f].astype(jnp.float32)
-            held[...] = both.astype(jnp.bfloat16)
+            held[...], _ = encode(decode_rows(held[...]) + decode_rows(p_pair[f]))
 
             @pl.when(f != mine)
             def _():
@@ -391,56 +413,85 @@
 
         each_member(g, add)
 
-    def dot_copy(k, slot, peer):
-        return pltpu.make_async_remote_copy(
-            src_ref=dots.at[k, slot],
-            dst_ref=dots.at[k, slot],
-            send_sem=dot_ss.at[k, peer],
-            recv_sem=dot_rs.at[k, slot],
+    def across_blocks(buf, ss, rs, k, slot, peer):
+        return pltpu.make_async_remote_copy(
+            src_ref=buf.at[k, slot],
+            dst_ref=buf.at[k, slot],
+            send_sem=ss.at[k, peer],
+            recv_sem=rs.at[k, slot],
             device_id=(me, peer),
+            device_id_type=MESH,
+        )
+
+    def across_samples(k, slot, peer):
+        return pltpu.make_async_remote_copy(
+            src_ref=sample_forms.at[k, slot],
+            dst_ref=sample_forms.at[k, slot],
+            send_sem=sf_ss.at[k, peer],
+            recv_sem=sf_rs.at[k, slot],
+            device_id=(peer, mv),
             device_id_type=MESH,
         )
 
     def each_block(action):
         loop(nv - 1, lambda i: action(lax.rem(mv + i + 1, nv)))
 
-    def send_dots(k):
+    def send_norm(k):
+        residual = res_ref[...]
+        norms[k, mv] = jnp.broadcast_to(row_sums(residual, residual), (kd, LANES))
+        each_block(lambda q: across_blocks(norms, norm_ss, norm_rs, k, mv, q).start())
+
+    def send_forms(k):
+        each_block(lambda q: across_blocks(block_forms, bf_ss, bf_rs, k, q, q).wait_recv())
+        sample_forms[k, me] = jnp.sum(block_forms[k], axis=0)
+        each_peer(lambda q: across_samples(k, me, q).start())
+
+    def norm_of(k):
+        each_block(lambda q: across_blocks(norms, norm_ss, norm_rs, k, q, q).wait_recv())
+        return jnp.sum(norms[k], axis=0)[:, 0:1]
+
+    def own_form(k):
+        each_peer(lambda q: across_samples(k, q, q).wait_recv())
+        forms = jnp.sum(sample_forms[k], axis=0)
+        row = lax.broadcasted_iota(jnp.int32, (kd, traits), 0)
+        column = lax.broadcasted_iota(jnp.int32, (kd, traits), 1)
+        found = jnp.zeros((kd, traits), jnp.float32)
+        for c in range(chunks):
+            wanted = me * kd + row - c * traits
+            found = found + jnp.where(column == wanted, forms[c, 0:1, :], 0.0)
+        return jnp.sum(found, axis=1, keepdims=True)
+
+    def update(k, before):
+        norm = norm_of(k)
+        form = own_form(k) * (1.0 / total_samples) + RIDGE * norm
         each_far(lambda f: p_copy(k, f, f).wait_recv())
-        linked = jnp.sum(p_recv[...].astype(jnp.float32), axis=0)
-        residual, direction = res_ref[...], dir_ref[...]
-        image = mask_row * linked + RIDGE * direction
-        link_ref[...] = linked
-        parts = (
-            row_sums(residual, residual),
-            row_sums(direction, image),
-            row_sums(residual, image),
-            row_sums(image, image),
-        )
-        packed = jnp.zeros((kd, LANES), jnp.float32)
-        for i, part in enumerate(parts):
-            packed = jnp.where(lane == i, part, packed)
-        dots[k, mv] = packed
-        each_block(lambda q: dot_copy(k, mv, q).start())
-
-    def update(k):
-        each_block(lambda q: dot_copy(k, q, q).wait_recv())
-        all_sums = jnp.sum(dots[k], axis=0)
-        norm, product, cross, image_norm = [all_sums[:, i : i + 1] for i in range(4)]
-        step = norm / product
-        direction, linked = dir_ref[...], link_ref[...]
+        linked = decode_rows(p_recv[0])
+        for f in range(1, pairs):
+            linked = linked + decode_rows(p_recv[f])
+        residual = res_ref[...]
+        if before is None:
+            step = norm / form
+            direction = residual
+        else:
+            last_norm, last_step = before
+            ratio = norm / last_norm
+            step = norm / (form - ratio * norm / last_step)
+            direction = residual + ratio * dir_ref[...]
+            linked = linked + ratio * link_ref[...]
         if k + 1 < ITERS:
             image = mask_row * linked + RIDGE * direction
-            residual = res_ref[...] - step * image
-            norm_next = norm - 2.0 * step * cross + step * step * image_norm
-            my_slot[...], dir_ref[...] = encode(residual + (norm_next / norm) * direction)
+            my_slot[...], res_ref[...] = encode(residual - step * image)
             start_gather(k + 1)
-            res_ref[...] = residual
+            send_norm(k + 1)
+            dir_ref[...] = direction
+            link_ref[...] = linked
             sol_ref[...] = sol_ref[...] + step * direction
             imp_ref[...] = imp_ref[...] + step * linked
         else:
             sol_ref[...] = sol_ref[...] + step * direction
             projected = imp_ref[...] + step * linked
             imp_ref[...] = jnp.where(mask_ref[...] == 1, z_ref[...], projected)
+        return norm, step
 
     def finish(k, g):
         each_member(g, lambda f: pair_copy(k, f, 1 - parity).wait_send())
@@ -451,15 +502,16 @@
                 p_copy(k, f, mine).wait_send()
 
         each_member(g, sent)
-
-        @pl.when(my_group == g)
-        def _():
-            each_block(lambda q: dot_copy(k, mv, q).wait_send())
+        each_block(lambda q: across_blocks(block_forms, bf_ss, bf_rs, k, mv, q).wait_send())
+        each_block(lambda q: across_blocks(norms, norm_ss, norm_rs, k, mv, q).wait_send())
+        each_peer(lambda q: across_samples(k, me, q).wait_send())
 
     def transpose(j):
         xt_ref[j] = x_ref[j].T
 
     groups = range(GROUPS)
+    before = None
+    send_norm(0)
     for k in range(ITERS):
         for g in groups:
             project(k, g)
@@ -469,12 +521,10 @@
             loop(tiles // 2, transpose)
         for g in groups:
             add_pairs(k, g)
+        send_forms(k)
         if k == 0:
             loop(tiles - tiles // 2, lambda j: transpose(tiles // 2 + j))
-        for g in groups:
-            pl.when(my_group == g)(functools.partial(send_dots, k))
-        for g in groups:
-            pl.when(my_group == g)(functools.partial(update, k))
+        before = update(k, before)
         for g in groups:
             finish(k, g)
 
@@ -507,10 +557,12 @@
             pltpu.VMEM((GROUPS, tiles, group_traits, ROWS), jnp.bfloat16),
             pltpu.VMEM((GROUPS, 2, tiles, group_traits, ROWS), jnp.bfloat16),
             pltpu.VMEM((group_traits, width), jnp.float32),
-            pltpu.VMEM((GROUPS, n // GROUPS, kd, width), jnp.bfloat16),
-            pltpu.VMEM((n // 2, kd, width), jnp.bfloat16),
-            pltpu.VMEM((n // 2, kd, width), jnp.bfloat16),
+            pltpu.VMEM((GROUPS, n // GROUPS, kd, width + LANES), jnp.int16),
+            pltpu.VMEM((n // 2, kd, width + LANES), jnp.int16),
+            pltpu.VMEM((n // 2, kd, width + LANES), jnp.int16),
             pltpu.VMEM((ITERS, nv, kd, LANES), jnp.float32),
+            pltpu.VMEM((ITERS, nv, n * kd // TRAITS, 8, TRAITS), jnp.float32),
+            pltpu.VMEM((ITERS, n, n * kd // TRAITS, 8, TRAITS), jnp.float32),
             dma((tiles,)),
             dma((n,)),
             dma((n,)),
@@ -524,6 +576,10 @@
             dma((ITERS, n // 2)),
             dma((ITERS, nv)),
             dma((ITERS, nv)),
+            dma((ITERS, nv)),
+            dma((ITERS, nv)),
+            dma((ITERS, n)),
+            dma((ITERS, n)),
         ],
         compiler_params=pltpu.CompilerParams(
             collective_id=0, has_side_effects=True, vmem_limit_bytes=56 << 20

time: 82.6 us -> 81.7 us (0.989)
  no operation moved by 1% of the time
where the time goes in v4:
time: 81.7 us; the launch traced here: 81.4 us
  Pallas kernels  77.8 us (95%)
  local copies, waits for them, and re-layouts  2.95 us (4%)
    pallas_call x1, Pallas kernels, on_device(): pl.pallas_call(functools.partial(kernel, n, nv), out_shape=(out, out), in...  77.8 us
    unnamed x2, local copies, waits for them, and re-layouts  2.95 us

profile of v4, /device:TPU:1, one launch (start us, length us, event | category | flops | bytes accessed | tf_op | source)
XLA Modules:
  0.0 81.4 jit_solution(6622974099526804412)
XLA Ops:
  0.6 77.8 %shard_map.50 = (f32[16,1024]{1,0:T(8,128)}, f32[16,1024]{1,0:T(8,128)}) custom-call(s32[1024,1024]{1,0:T(8,128)} %g_hbm.1, s32[1,1024]{1,0:T(1,128)} %bitcast.1, f32[16,1024]{1,0:T(8,128)} %z_ref.1), custom_call_target="tpu_custom_call" | custom-call | tf_op jit(solution)/shard_map/pallas_call | solution.py:541
  78.5 1.5 %copy.7 = f32[16,1024]{1,0:T(8,128)} copy(f32[16,1024]{1,0:T(8,128)} %get-tuple-element.4) | data formatting | bytes 131072
  80.0 1.5 %copy.8 = f32[16,1024]{1,0:T(8,128)} copy(f32[16,1024]{1,0:T(8,128)} %get-tuple-element.5) | data formatting | bytes 131072

commit v5 on v4

--- a/solution.py
+++ b/solution.py
@@ -79,6 +79,7 @@
     t_own,
     t_side,
     p_acc,
+    form_acc,
     p_send,
     p_pair,
     p_recv,
@@ -349,17 +350,11 @@
                     jnp.float32
                 )
                 mixed = t_own[g, j, at].astype(jnp.float32) + 0.5 * sides
-                forms = lax.dot_general(
-                    jnp.ones((8, ROWS), jnp.bfloat16),
-                    split_high_low(t_own[g, j, at].astype(jnp.float32) * mixed),
-                    (((1,), (1,)), ((), ())),
-                    preferred_element_type=jnp.float32,
-                )
-                form = forms[:, :traits] + forms[:, traits:]
+                product = t_own[g, j, at].astype(jnp.float32) * mixed
                 if isinstance(j, int) and j == 0:
-                    block_forms[k, mv, c] = form
+                    form_acc[at] = product
                 else:
-                    block_forms[k, mv, c] = block_forms[k, mv, c] + form
+                    form_acc[at] = form_acc[at] + product
                 part = jnp.dot(
                     mixed.astype(jnp.bfloat16), x_ref[j], preferred_element_type=jnp.float32
                 )
@@ -372,7 +367,7 @@
 
         if tiles > 4:
             p_acc[...] = jnp.zeros_like(p_acc)
-            block_forms[k, mv] = jnp.zeros(block_forms.shape[2:], jnp.float32)
+            form_acc[...] = jnp.zeros_like(form_acc)
         loop(tiles, back)
 
         def to_send(c):
@@ -384,6 +379,17 @@
         loop(chunks, to_send)
         gather_sent(k, g)
         each_member(g, lambda f: pair_copy(k, f, 1 - parity).start())
+
+        def sum_forms(c):
+            forms = lax.dot_general(
+                jnp.ones((8, ROWS), jnp.bfloat16),
+                split_high_low(form_acc[rows_at(c)]),
+                (((1,), (1,)), ((), ())),
+                preferred_element_type=jnp.float32,
+            )
+            block_forms[k, mv, c] = forms[:, :traits] + forms[:, traits:]
+
+        loop(chunks, sum_forms)
         each_block(lambda q: across_blocks(block_forms, bf_ss, bf_rs, k, mv, q).start())
 
         def t_sent(j):
@@ -557,6 +563,7 @@
             pltpu.VMEM((GROUPS, tiles, group_traits, ROWS), jnp.bfloat16),
             pltpu.VMEM((GROUPS, 2, tiles, group_traits, ROWS), jnp.bfloat16),
             pltpu.VMEM((group_traits, width), jnp.float32),
+            pltpu.VMEM((group_traits, ROWS), jnp.float32),
             pltpu.VMEM((GROUPS, n // GROUPS, kd, width + LANES), jnp.int16),
             pltpu.VMEM((n // 2, kd, width + LANES), jnp.int16),
             pltpu.VMEM((n // 2, kd, width + LANES), jnp.int16),

time: 81.7 us -> 81.7 us (level)
  no operation moved by 1% of the time
where the time goes in v5:
time: 81.7 us; the launch traced here: 81.4 us
  Pallas kernels  77.8 us (95%)
  local copies, waits for them, and re-layouts  2.95 us (4%)
    pallas_call x1, Pallas kernels, on_device(): pl.pallas_call(functools.partial(kernel, n, nv), out_shape=(out, out), in...  77.8 us
    unnamed x2, local copies, waits for them, and re-layouts  2.95 us

profile of v5, /device:TPU:1, one launch (start us, length us, event | category | flops | bytes accessed | tf_op | source)
XLA Modules:
  0.0 81.4 jit_solution(12853287526126673280)
XLA Ops:
  0.6 77.8 %shard_map.50 = (f32[16,1024]{1,0:T(8,128)}, f32[16,1024]{1,0:T(8,128)}) custom-call(s32[1024,1024]{1,0:T(8,128)} %g_hbm.1, s32[1,1024]{1,0:T(1,128)} %bitcast.1, f32[16,1024]{1,0:T(8,128)} %z_ref.1), custom_call_target="tpu_custom_call" | custom-call | tf_op jit(solution)/shard_map/pallas_call | solution.py:547
  78.5 1.5 %copy.7 = f32[16,1024]{1,0:T(8,128)} copy(f32[16,1024]{1,0:T(8,128)} %get-tuple-element.4) | data formatting | bytes 131072
  79.9 1.5 %copy.8 = f32[16,1024]{1,0:T(8,128)} copy(f32[16,1024]{1,0:T(8,128)} %get-tuple-element.5) | data formatting | bytes 131072
